TPU v7x, 256 devices: a whole 4x4x8 slice. The times are simulated.
256 devices in a mesh: vp: 64 (over y_hi, z, x), ch: 4 (over y_lo, core).
Axes of the slice: x: 4, y: 4 (y_hi: 2, y_lo: 2; y = y_hi * 2 + y_lo), z: 8, core: 2. Of those that a mesh axis runs over, the one named last changes fastest.
Arguments:
- chol_a: bfloat16 [640, 4, 6000], P('vp', None, 'ch'), may hold values from -0.078125 to 0.078125
- chol_b: bfloat16 [6000, 64, 640], P('ch', 'vp'), may hold values from -6 to 6
- amplitudes: bfloat16 [640, 8, 640], P('vp'), may hold values from -0.0390625 to 0.0390625
- vir_a: float32 [4], replicated, may hold values from 0.2 to 3
- vir_b: float32 [64], P('vp'), may hold values from 0.2 to 3
- occ_pair: float32 [8], P('ch'), may hold values from -4 to -1
Outputs:
- increment: float32 [4, 64, 8], P(None, 'vp', 'ch')
All inputs are finite; a program needn't handle non-finite values.
Results may differ from a plain program's by a relative error of at most 0.0029.
Values may be sent and summed in bfloat16 or wider, within the bound.
A program may use at most 64 MiB of HBM per device.

v0:
```python
import jax
import jax.numpy as jnp
from jax import lax
from jax.sharding import PartitionSpec as P


def body(chol_a, chol_b, amplitudes, vir_a, vir_b, occ_pair):
    nch_dev = chol_b.shape[0]
    nb_dev = chol_b.shape[1]
    vir_count = chol_b.shape[2]
    a_count = chol_a.shape[1]
    pair_count = amplitudes.shape[1]
    cholesky_right = chol_b.reshape(nch_dev, nb_dev * vir_count)
    panel_rows = lax.all_gather(chol_a, "vp", axis=0, tiled=True)
    rows_here = panel_rows.shape[0]
    v_rows = jnp.dot(
        panel_rows.reshape(rows_here * a_count, nch_dev),
        cholesky_right,
        preferred_element_type=jnp.float32,
    )
    v_all = v_rows.astype(jnp.bfloat16).reshape(rows_here, a_count * nb_dev, vir_count)
    v_rows = v_all
    ladder = jnp.einsum(
        "cxd,cid->xi",
        v_rows,
        lax.all_gather(amplitudes, "vp", axis=0, tiled=True),
        preferred_element_type=jnp.float32,
    )
    ladder = ladder.reshape(a_count, nb_dev, pair_count)
    ladder = lax.psum_scatter(ladder, "ch", scatter_dimension=2, tiled=True)
    energy_gap = vir_a[:, None, None] + vir_b[None, :, None] - occ_pair[None, None, :]
    return ladder / energy_gap


def solution(mesh):
    return jax.shard_map(
        body,
        mesh=mesh,
        in_specs=(
            P("vp", None, "ch"),
            P("ch", "vp", None),
            P("vp", None, None),
            P(),
            P("vp"),
            P("ch"),
        ),
        out_specs=P(None, "vp", "ch"),
        check_vma=False,
    )
```

profile of v0, /device:TPU:1, one launch (start us, length us, event | category | flops | bytes accessed | tf_op | source)
XLA Modules:
  0.0 319.8 jit_solution(13884789636193917193)
XLA Ops:
  6.5 0.0 copy-start
  6.5 0.0 all-gather.3.cloned.1.call-start
  6.5 0.7 all-gather.3.cloned.1.call-update
  7.3 0.0 all-gather.5.cloned.1.call-start
  7.3 0.7 all-gather.5.cloned.1.call-update
  8.7 1.3 dynamic-slice
  10.6 0.7 broadcast_add_fusion
  11.2 145.8 %all-gather.3.cloned.1.call-done = bf16[640,4,1500]{2,1,0:T(4,128)(2,1)} async-done(((bf16[10,4,1500]{2,1,0:T(4,128)(2,1)}), bf16[640,4,1500]{2,1,0:T(4,128)(2,1)}) %all-gather.3.cloned.1.call-update) | async-done | bytes 7680016 | tf_op jit(solution)/shard_map/all_gather | solution.py:14
  157.0 13.2 %reshape.60 = bf16[2560,1500]{1,0:T(8,128)(2,1)} reshape(bf16[640,4,1500]{2,1,0:T(4,128)(2,1)} %all-gather.3.cloned.1.call-done) | data formatting | bytes 15360000 | tf_op jit(solution)/shard_map/reshape | solution.py:17
  170.2 0.0 copy-done
  170.2 9.7 %convolution_convert_fusion = bf16[2560,640]{1,0:T(8,128)(2,1)} fusion(bf16[2560,1500]{1,0:T(8,128)(2,1)} %reshape.60, bf16[1500,1,640]{2,0,1:T(8,128)(2,1)S(1)} %copy-done), kind=kOutput, calls=%fused_computation | convolution fusion | flops 4916838400 | bytes 12876800 | tf_op jit(solution)/shard_map/dot_general | solution.py:16
  180.0 6.5 %reshape.62 = bf16[640,4,640]{2,1,0:T(4,128)(2,1)} reshape(bf16[2560,640]{1,0:T(8,128)(2,1)} %convolution_convert_fusion) | data formatting | bytes 6553600 | tf_op jit(solution)/shard_map/reshape | solution.py:21
  186.5 0.0 copy-start.1
  186.5 108.7 %all-gather.5.cloned.1.call-done = bf16[640,8,640]{2,1,0:T(8,128)(2,1)} async-done(((bf16[10,8,640]{2,1,0:T(8,128)(2,1)}), bf16[640,8,640]{2,1,0:T(8,128)(2,1)}) %all-gather.5.cloned.1.call-update) | async-done | bytes 6553616 | tf_op jit(solution)/shard_map/all_gather | solution.py:26
  295.2 8.2 %fusion.1 = f32[4,8,1]{0,1,2:T(8,128)S(1)} fusion(bf16[640,4,640]{2,1,0:T(4,128)(2,1)} %reshape.62, bf16[640,8,640]{2,1,0:T(8,128)(2,1)} %all-gather.5.cloned.1.call-done), kind=kOutput, calls=%fused_computation.5 | convolution fusion | flops 26214400 | bytes 9830528 | tf_op jit(solution)/shard_map/cxd,cid->xi/dot_general | solution.py:23
  303.3 9.0 %all-reduce = f32[4,1,8]{0,1,2:T(1,128)S(1)} all-reduce(f32[4,1,8]{0,1,2:T(1,128)S(1)} %bitcast.14), channel_id=2, replica_groups=mesh['vp'=64,'ch'=4] {'ch'}, use_global_device_ids=true, to_apply=%region_0.0.clone | all-reduce | flops 32 | bytes 256
  312.3 0.0 copy-done.1
  312.3 0.6 subtract_divide_fusion
  (1 shorter events, 0.0 us)
Async XLA Ops:
  6.5 163.7 %copy-start = (bf16[1500,1,640]{2,0,1:T(8,128)(2,1)S(1)}, bf16[1500,1,640]{2,0,1:T(8,128)(2,1)}, u32[]{:S(2)}) copy-start(bf16[1500,1,640]{2,0,1:T(8,128)(2,1)} %param.7) | copy-start | bytes 5760004
  6.5 150.5 %all-gather.3.cloned.1.call-start = ((), (), s32[]{:S(2)}) async-start(), calls=%async_computation | async-start | bytes 7987200 | tf_op jit(solution)/shard_map/all_gather | solution.py:14
  7.3 287.9 %all-gather.5.cloned.1.call-start = ((), (), s32[]{:S(2)}) async-start(), calls=%async_computation.1 | async-start | bytes 6656000 | tf_op jit(solution)/shard_map/all_gather | solution.py:26
  186.5 125.9 %copy-start.1 = (f32[2]{0:T(128)S(1)}, f32[2]{0:T(128)}, u32[]{:S(2)}) copy-start(f32[2]{0:T(128)} %param.11) | copy-start | bytes 28
Sparse Core Ops, SparseCore 0:
  11.0 145.9 all-gather.2
  160.5 134.6 all-gather.4
where the time goes:
time: 320 us
  waiting for transfers between devices  256 us (80%)
  local copies, waits for them, and re-layouts  21 us (7%)
  matrix products  17.9 us (6%)
  between operations  14.7 us (5%)
  blocking collectives  8.96 us (3%)
    all_gather x1, waiting for transfers between devices, body(): panel_rows = lax.all_gather(chol_a, 'vp', axis=0, tiled=True)  146 us
    all_gather x1, waiting for transfers between devices, body(): lax.all_gather(amplitudes, 'vp', axis=0, tiled=True)  109 us
    reshape x1, local copies, waits for them, and re-layouts, body(): panel_rows.reshape(rows_here * a_count, nch_dev)  13.2 us
    dot_general x1, matrix products, body(): jnp.dot(panel_rows.reshape(rows_here * a_count, nch_dev), cholesky_right,...  9.73 us
    unnamed x1, blocking collectives  8.96 us
    dot_general x1, matrix products, body(): jnp.einsum('cxd,cid->xi', v_rows, lax.all_gather(amplitudes, 'vp', axis=0...  8.17 us
    reshape x1, local copies, waits for them, and re-layouts, body(): v_rows.astype(jnp.bfloat16).reshape(rows_here, a_count * nb_dev, vir_count)  6.49 us
  transfers between devices with their start and end apart: 2, of which 2 were waited for; matrix products, arithmetic and copies ran while one was open for 10% of the time, Pallas kernels for 0%

commit v1 on v0

--- a/solution.py
+++ b/solution.py
@@ -23,7 +23,9 @@
     ladder = jnp.einsum(
         "cxd,cid->xi",
         v_rows,
-        lax.all_gather(amplitudes, "vp", axis=0, tiled=True),
+        jnp.concatenate(
+            lax.all_to_all(jnp.stack([amplitudes] * lax.axis_size("vp")), "vp", 0, 0), axis=0
+        ),
         preferred_element_type=jnp.float32,
     )
     ladder = ladder.reshape(a_count, nb_dev, pair_count)

time: 320 us -> 264 us (0.82)
  waiting for transfers between devices: 256 us -> 182 us
  starting transfers between devices: 0.04 us -> 15.5 us
  local copies, waits for them, and re-layouts: 21 us -> 24.5 us
    all_gather x1 -> x0, waiting for transfers between devices: 109 us -> none  [body(): lax.all_gather(amplitudes, 'vp', axis=0, tiled=True)]
    all_gather x1, waiting for transfers between devices: 146 us -> 181 us  [body(): panel_rows = lax.all_gather(chol_a, 'vp', axis=0, tiled=True)]
    all_to_all x0 -> x1, starting transfers between devices: none -> 15.5 us  [body(): lax.all_to_all(jnp.stack([amplitudes] * lax.axis_size('vp')), 'vp', 0, 0)]
    another operation x0 -> x1, local copies, waits for them, and re-layouts: none -> 4.14 us  [body(): jnp.stack([amplitudes] * lax.axis_size('vp'))]
  transfers between devices with their start and end apart: 2 -> 2, of which waited for: 2 -> 1; matrix products, arithmetic and copies ran while one was open for 10% -> 13% of each run, Pallas kernels for 0% -> 0%
where the time goes in v1:
time: 264 us; the launch traced here: 262 us
  waiting for transfers between devices  182 us (69%)
  local copies, waits for them, and re-layouts  24.5 us (9%)
  matrix products  18 us (7%)
  starting transfers between devices  15.5 us (6%)
  between operations  14.7 us (6%)
  blocking collectives  6.74 us (3%)
    all_gather x1, waiting for transfers between devices, body(): panel_rows = lax.all_gather(chol_a, 'vp', axis=0, tiled=True)  181 us
    all_to_all x1, starting transfers between devices, body(): lax.all_to_all(jnp.stack([amplitudes] * lax.axis_size('vp')), 'vp', 0, 0)  15.5 us
    reshape x1, local copies, waits for them, and re-layouts, body(): panel_rows.reshape(rows_here * a_count, nch_dev)  13.2 us
    dot_general x1, matrix products, body(): jnp.dot(panel_rows.reshape(rows_here * a_count, nch_dev), cholesky_right,...  9.78 us
    dot_general x1, matrix products, body(): jnp.einsum('cxd,cid->xi', v_rows, jnp.concatenate(lax.all_to_all(jnp.stac...  8.17 us
    unnamed x1, blocking collectives  6.74 us
    reshape x1, local copies, waits for them, and re-layouts, body(): v_rows.astype(jnp.bfloat16).reshape(rows_here, a_count * nb_dev, vir_count)  6.49 us
  transfers between devices with their start and end apart: 2, of which 1 were waited for; matrix products, arithmetic and copies ran while one was open for 13% of the time, Pallas kernels for 0%

profile of v1, /device:TPU:1, one launch (start us, length us, event | category | flops | bytes accessed | tf_op | source)
XLA Modules:
  0.0 262.0 jit_solution(14730057927409799869)
XLA Ops:
  6.5 0.0 copy-start
  6.5 0.0 all-gather.2.cloned.1.call-start
  6.5 0.7 all-gather.2.cloned.1.call-update
  7.3 4.1 %stack.2 = bf16[64,10,8,640]{3,2,1,0:T(8,128)(2,1)} broadcast(bf16[10,8,640]{2,1,0:T(8,128)(2,1)} %param.8), dimensions={1,2,3} | broadcast | bytes 6656000 | tf_op jit(solution)/shard_map/stack | solution.py:27
  11.4 0.0 copy-start.3
  11.4 0.0 copy-start.2
  11.4 15.5 %all-to-all-start = ((bf16[64,10,8,640]{3,2,1,0:T(8,128)(2,1)}), bf16[64,10,8,640]{3,2,1,0:T(8,128)(2,1)}, u32[]{:S(2)}, u32[]{:S(2)}) async-start(bf16[64,10,8,640]{3,2,1,0:T(8,128)(2,1)} %stack.2), calls=%async_computation | async-start | bytes 13107200 | tf_op jit(solution)/shard_map/all_to_all | solution.py:27
  27.5 0.0 copy-done.3
  27.6 0.6 dynamic-slice
  28.8 0.0 copy-done.2
  28.8 181.2 %all-gather.2.cloned.1.call-done = bf16[640,4,1500]{2,1,0:T(4,128)(2,1)} async-done(((bf16[10,4,1500]{2,1,0:T(4,128)(2,1)}), bf16[640,4,1500]{2,1,0:T(4,128)(2,1)}) %all-gather.2.cloned.1.call-update) | async-done | bytes 7680016 | tf_op jit(solution)/shard_map/all_gather | solution.py:14
  210.1 13.2 %reshape.65 = bf16[2560,1500]{1,0:T(8,128)(2,1)} reshape(bf16[640,4,1500]{2,1,0:T(4,128)(2,1)} %all-gather.2.cloned.1.call-done) | data formatting | bytes 15360000 | tf_op jit(solution)/shard_map/reshape | solution.py:17
  223.3 0.0 copy-done
  223.3 9.8 %convolution_convert_fusion = bf16[2560,640]{1,0:T(8,128)(2,1)} fusion(bf16[2560,1500]{1,0:T(8,128)(2,1)} %reshape.65, bf16[1500,1,640]{2,0,1:T(8,128)(2,1)S(1)} %copy-done), kind=kOutput, calls=%fused_computation | convolution fusion | flops 4916838400 | bytes 12876800 | tf_op jit(solution)/shard_map/dot_general | solution.py:16
  233.1 6.5 %reshape.67 = bf16[640,4,640]{2,1,0:T(4,128)(2,1)} reshape(bf16[2560,640]{1,0:T(8,128)(2,1)} %convolution_convert_fusion) | data formatting | bytes 6553600 | tf_op jit(solution)/shard_map/reshape | solution.py:21
  239.6 0.0 copy-start.1
  239.6 0.0 all-to-all-done
  239.6 8.2 %fusion.1 = f32[4,8,1]{0,1,2:T(8,128)S(1)} fusion(bf16[640,4,640]{2,1,0:T(4,128)(2,1)} %reshape.67, bf16[640,8,640]{2,1,0:T(8,128)(2,1)} %bitcast.1), kind=kOutput, calls=%fused_computation.5 | convolution fusion | flops 26214400 | bytes 9830528 | tf_op jit(solution)/shard_map/cxd,cid->xi/dot_general | solution.py:23
  247.7 6.7 %all-reduce = f32[4,1,8]{0,1,2:T(1,128)S(1)} all-reduce(f32[4,1,8]{0,1,2:T(1,128)S(1)} %bitcast.15), channel_id=2, replica_groups=mesh['vp'=64,'ch'=4] {'ch'}, use_global_device_ids=true, to_apply=%region_0.0.clone | all-reduce | flops 32 | bytes 256
  254.5 0.0 copy-done.1
  254.5 0.6 subtract_divide_fusion
  (2 shorter events, 0.0 us)
Async XLA Ops:
  6.5 216.7 %copy-start = (bf16[1500,1,640]{2,0,1:T(8,128)(2,1)S(1)}, bf16[1500,1,640]{2,0,1:T(8,128)(2,1)}, u32[]{:S(2)}) copy-start(bf16[1500,1,640]{2,0,1:T(8,128)(2,1)} %param.7) | copy-start | bytes 5760004
  6.5 203.5 %all-gather.2.cloned.1.call-start = ((), (), s32[]{:S(2)}) async-start(), calls=%async_computation.1 | async-start | bytes 7987200 | tf_op jit(solution)/shard_map/all_gather | solution.py:14
  11.4 16.1 %copy-start.3 = (u32[256]{0:T(256)S(1)}, u32[256]{0:T(256)}, u32[]{:S(2)}) copy-start(u32[256]{0:T(256)} %constant.7) | copy-start | bytes 3076
  11.4 17.4 %copy-start.2 = (f32[4]{0:T(128)S(1)}, f32[4]{0:T(128)}, u32[]{:S(2)}) copy-start(f32[4]{0:T(128)} %param.9) | copy-start | bytes 52
  11.4 228.1 %all-to-all-start = ((bf16[64,10,8,640]{3,2,1,0:T(8,128)(2,1)}), bf16[64,10,8,640]{3,2,1,0:T(8,128)(2,1)}, u32[]{:S(2)}, u32[]{:S(2)}) async-start(bf16[64,10,8,640]{3,2,1,0:T(8,128)(2,1)} %stack.2), calls=%async_computation | async-start | bytes 13107200 | tf_op jit(solution)/shard_map/all_to_all | solution.py:27
  239.6 14.9 %copy-start.1 = (f32[2]{0:T(128)S(1)}, f32[2]{0:T(128)}, u32[]{:S(2)}) copy-start(f32[2]{0:T(128)} %param.11) | copy-start | bytes 28
Sparse Core Ops, SparseCore 0:
  11.0 198.9 all-gather.1
